TPU v7x, 1024 devices: a whole 4x4x32 slice. The times are simulated.
1024 devices in a mesh: pipe: 16 (over x, z_hi), dp: 8 (over z_lo), tensor: 8 (over y, core).
Axes of the slice: x: 4, y: 4, z: 32 (z_hi: 4, z_lo: 8; z = z_hi * 8 + z_lo), core: 2. Of those that a mesh axis runs over, the one named last changes fastest.
Arguments:
- section_out: bfloat16 [16, 1024, 2048], P('pipe', 'dp'), may hold values from -6 to 6
- section_grad: bfloat16 [16, 1024, 2048], P('pipe', 'dp'), may hold values from -6 to 6
- hosted: bfloat16 [16, 2, 1024, 2048], P('pipe', None, 'dp'), may hold values from -6 to 6
- send_slot: int32 [16], P('pipe'), may hold values from 0 to 1
- gain: float32 [16, 2048], P('pipe'), may hold values from 0.5 to 1.5
- w_up: bfloat16 [16, 2048, 6144], P('pipe', None, 'tensor'), may hold values from -0.125 to 0.125
- w_down: bfloat16 [16, 6144, 2048], P('pipe', 'tensor'), may hold values from -0.078125 to 0.078125
Outputs:
- next_forward: bfloat16 [16, 1024, 2048], P('pipe', 'dp')
- next_backward: bfloat16 [16, 1024, 2048], P('pipe', 'dp')
- to_host: bfloat16 [16, 1024, 2048], P('pipe', 'dp')
- gain_grad: float32 [16, 2048], P('pipe')
All inputs are finite; a program needn't handle non-finite values.
Results may differ from a plain program's by a relative error of at most 0.015.
Values may be sent and summed in bfloat16 or wider, within the bound.
A program may use at most 64 MiB of HBM per device.

v0:
```python
import jax
import jax.numpy as jnp
from jax import lax
from jax.sharding import PartitionSpec as P

epsilon = 1e-05


def shifted(block, axis, distance):
    devices = range(lax.axis_size(axis))
    route = [((i - distance) % len(devices), i) for i in devices]
    return lax.ppermute(block, axis, route)


def normalize(activation):
    values = activation.astype(jnp.float32)
    factor = lax.rsqrt(jnp.mean(values * values, axis=-1, keepdims=True) + epsilon)
    return (values * factor, factor)


def silu_slope(pre):
    sigma = jax.nn.sigmoid(pre)
    return sigma * (1.0 + pre * (1.0 - sigma))


def body(section_out, section_grad, hosted, send_slot, gain, w_up, w_down):
    forward_in = shifted(section_out, "pipe", 1)[0]
    incoming = shifted(section_grad, "pipe", -1)[0]
    chosen = lax.dynamic_index_in_dim(hosted[0], send_slot[0], 0, keepdims=False)
    outgoing, returning = (forward_in, chosen)
    sections = lax.axis_size("pipe")
    first_flat = outgoing.reshape(sections, -1)
    second_flat = returning.reshape(sections, -1)
    spread_first, spread_second = (
        lax.all_to_all(first_flat, "pipe", split_axis=0, concat_axis=0, tiled=True),
        lax.all_to_all(second_flat, "pipe", split_axis=0, concat_axis=0, tiled=True),
    )
    back_first, back_second = (
        lax.all_to_all(spread_first[::-1], "pipe", split_axis=0, concat_axis=0, tiled=True),
        lax.all_to_all(spread_second[::-1], "pipe", split_axis=0, concat_axis=0, tiled=True),
    )
    payload = (back_first.reshape(outgoing.shape), back_second.reshape(returning.shape))
    arrived, fetched = payload
    weights_up = w_up[0]
    weights_down = w_down[0]
    gains = gain[0]
    forward_hat = normalize(forward_in)[0]
    normed = (forward_hat * gains).astype(jnp.bfloat16)
    hidden = jax.nn.silu(jnp.dot(normed, weights_up, preferred_element_type=jnp.float32)).astype(
        jnp.bfloat16
    )
    mixed_part = jnp.dot(hidden, weights_down, preferred_element_type=jnp.float32)
    saved_hat, saved_factor = normalize(fetched)
    saved_normed = (saved_hat * gains).astype(jnp.bfloat16)
    saved_pre = jnp.dot(saved_normed, weights_up, preferred_element_type=jnp.float32)
    hidden_grad = jnp.dot(incoming, weights_down.T, preferred_element_type=jnp.float32)
    pre_grad = (hidden_grad * silu_slope(saved_pre)).astype(jnp.bfloat16)
    grad_part = jnp.dot(pre_grad, weights_up.T, preferred_element_type=jnp.float32)
    mixed, normed_grad = (
        lax.psum(mixed_part.astype(jnp.bfloat16), "tensor").astype(jnp.float32),
        lax.psum(grad_part.astype(jnp.bfloat16), "tensor").astype(jnp.float32),
    )
    next_forward = (forward_in.astype(jnp.float32) + mixed).astype(jnp.bfloat16)
    hat_grad = normed_grad * gains
    input_grad = saved_factor * (
        hat_grad - saved_hat * jnp.mean(hat_grad * saved_hat, axis=-1, keepdims=True)
    )
    next_backward = (incoming.astype(jnp.float32) + input_grad).astype(jnp.bfloat16)
    gain_total = lax.psum(jnp.sum(normed_grad * saved_hat, axis=0), "dp")
    return (next_forward[None], next_backward[None], arrived[None], gain_total[None])


def solution(mesh):
    placed = (
        P("pipe", "dp", None),
        P("pipe", "dp", None),
        P("pipe", None, "dp", None),
        P("pipe"),
        P("pipe", None),
        P("pipe", None, "tensor"),
        P("pipe", "tensor", None),
    )
    return jax.shard_map(
        body,
        mesh=mesh,
        in_specs=placed,
        out_specs=(
            P("pipe", "dp", None),
            P("pipe", "dp", None),
            P("pipe", "dp", None),
            P("pipe", None),
        ),
        check_vma=False,
    )
```

profile of v0, /device:TPU:2, one launch (start us, length us, event | category | flops | bytes accessed | tf_op | source)
XLA Modules:
  0.0 652.8 jit_solution(1882460789996777191)
XLA Ops:
  8.0 2.0 constant_dynamic-slice_fusion
  10.0 3.6 all_to_all.38
  13.7 0.5 broadcast.75
  14.2 5.7 reduce.5
  19.9 2.2 reshape.97
  22.1 31.3 %all-to-all-start = ((bf16[16,2,8192]{2,1,0:T(2,128)(2,1)}), bf16[16,2,8192]{2,1,0:T(2,128)(2,1)}, u32[]{:S(2)}, u32[]{:S(2)}) async-start(bf16[16,2,8192]{2,1,0:T(2,128)(2,1)} %reshape.97), calls=%async_computation | async-start | bytes 1048576 | tf_op jit(solution)/shard_map/all_to_all | solution.py:36
  53.5 12.1 %collective-permute-start = (bf16[1,128,2048]{2,1,0:T(8,128)(2,1)}, bf16[1,128,2048]{2,1,0:T(8,128)(2,1)}, u32[]{:S(2)}, u32[]{:S(2)}) collective-permute-start(bf16[1,128,2048]{2,1,0:T(8,128)(2,1)} %param.7), channel_id=1, source_target_pairs={{960,0},{0,64},{64,128},{128,192},{192,256},{256,320},{320,384},{3... | collective-permute-start | bytes 1572872 | tf_op jit(solution)/shard_map/ppermute | solution.py:12
  65.5 33.0 %collective-permute-done = bf16[1,128,2048]{2,1,0:T(8,128)(2,1)} collective-permute-done((bf16[1,128,2048]{2,1,0:T(8,128)(2,1)}, bf16[1,128,2048]{2,1,0:T(8,128)(2,1)}, u32[]{:S(2)}, u32[]{:S(2)}) %collective-permute-start) | collective-permute-done | bytes 524320 | tf_op jit(solution)/shard_map/ppermute | solution.py:12
  98.6 3.6 all_to_all.39
  102.2 5.7 reduce.7
  107.9 2.2 reshape.101
  110.1 14.9 %all-to-all-start.2 = ((bf16[16,2,8192]{2,1,0:T(2,128)(2,1)}), bf16[16,2,8192]{2,1,0:T(2,128)(2,1)}, u32[]{:S(2)}, u32[]{:S(2)}) async-start(bf16[16,2,8192]{2,1,0:T(2,128)(2,1)} %reshape.101), calls=%async_computation.2 | async-start | bytes 1048576 | tf_op jit(solution)/shard_map/all_to_all | solution.py:35
  125.0 3.5 reshape.98
  128.5 2.6 copy.24
  131.1 55.4 %rev.6 = bf16[16,16384]{1,0:T(8,128)(2,1)} reverse(bf16[16,16384]{1,0:T(8,128)(2,1)} %bitcast.74), dimensions={0} | reverse | bytes 1048576 | tf_op jit(solution)/shard_map/rev | solution.py:40
  186.5 2.7 reduce.6
  189.2 2.2 reshape.99
  191.4 25.9 %all-to-all-done.2 = bf16[16,2,8192]{2,1,0:T(2,128)(2,1)} async-done(((bf16[16,2,8192]{2,1,0:T(2,128)(2,1)}), bf16[16,2,8192]{2,1,0:T(2,128)(2,1)}, u32[]{:S(2)}, u32[]{:S(2)}) %all-to-all-start.2) | async-done | bytes 524320 | tf_op jit(solution)/shard_map/all_to_all | solution.py:35
  217.3 15.1 %all-to-all-start.1 = ((bf16[16,2,8192]{2,1,0:T(2,128)(2,1)}), bf16[16,2,8192]{2,1,0:T(2,128)(2,1)}, u32[]{:S(2)}, u32[]{:S(2)}) async-start(bf16[16,2,8192]{2,1,0:T(2,128)(2,1)} %reshape.99), calls=%async_computation.1 | async-start | bytes 1048576 | tf_op jit(solution)/shard_map/all_to_all | solution.py:40
  232.5 3.5 reshape.102
  235.9 2.6 copy.23
  238.5 55.4 %rev.7 = bf16[16,16384]{1,0:T(8,128)(2,1)} reverse(bf16[16,16384]{1,0:T(8,128)(2,1)} %bitcast.75), dimensions={0} | reverse | bytes 1048576 | tf_op jit(solution)/shard_map/rev | solution.py:39
  294.0 2.7 reduce.8
  296.7 2.2 reshape.103
  298.9 24.0 %all-to-all-start.3 = ((bf16[16,2,8192]{2,1,0:T(2,128)(2,1)}), bf16[16,2,8192]{2,1,0:T(2,128)(2,1)}, u32[]{:S(2)}, u32[]{:S(2)}) async-start(bf16[16,2,8192]{2,1,0:T(2,128)(2,1)} %reshape.103), calls=%async_computation.3 | async-start | bytes 1048576 | tf_op jit(solution)/shard_map/all_to_all | solution.py:39
  323.0 12.3 %collective-permute-start.1 = (bf16[1,128,2048]{2,1,0:T(8,128)(2,1)}, bf16[1,128,2048]{2,1,0:T(8,128)(2,1)}, u32[]{:S(2)}, u32[]{:S(2)}) collective-permute-start(bf16[1,128,2048]{2,1,0:T(8,128)(2,1)} %param.8), channel_id=1, source_target_pairs={{64,0},{128,64},{192,128},{256,192},{320,256},{384,320},{448,384},... | collective-permute-start | bytes 1572872 | tf_op jit(solution)/shard_map/ppermute | solution.py:12
  335.3 1.2 fusion.31
  336.6 4.2 fusion.13
  340.7 3.5 reshape.100
  344.2 5.2 convert_reduce_fusion
  349.4 2.4 reshape.93
  351.8 1.4 multiply_reduce_fusion
  353.2 0.1 rsqrt.22
  353.3 1.1 mul.112
  354.4 3.5 mul.113
  357.9 5.8 fusion.37
  363.7 2.1 convert_element_type.80
  365.8 1.6 fusion.6
  367.4 24.7 %collective-permute-done.1 = bf16[1,128,2048]{2,1,0:T(8,128)(2,1)} collective-permute-done((bf16[1,128,2048]{2,1,0:T(8,128)(2,1)}, bf16[1,128,2048]{2,1,0:T(8,128)(2,1)}, u32[]{:S(2)}, u32[]{:S(2)}) %collective-permute-start.1) | collective-permute-done | bytes 524320 | tf_op jit(solution)/shard_map/ppermute | solution.py:12
  392.1 5.2 fusion.10
  397.3 196.9 %all-reduce.3.cloned.1.call-done = (bf16[128,2048]{1,0:T(8,128)(2,1)}, bf16[128,2048]{1,0:T(8,128)(2,1)}) async-done(((bf16[128,2048]{1,0:T(8,128)(2,1)}, bf16[128,2048]{1,0:T(8,128)(2,1)}), (bf16[128,2048]{1,0:T(8,128)(2,1)}, bf16[128,2048]{1,0:T(8,128)(2,1)})) %all-reduce.3.cloned.1.call-update) | async-done | bytes 1048592 | tf_op jit(solution)/shard_map/psum | solution.py:60
  594.1 1.8 fusion.30
  595.9 34.6 %psum.23 = f32[1,2048]{1,0:T(1,128)} all-reduce(f32[1,2048]{1,0:T(1,128)S(1)} %bitcast.83), channel_id=1, replica_groups=mesh['pipe'=16,'dp'=8,'tensor'=8] {'dp'}, use_global_device_ids=true, to_apply=%region_6.7 | all-reduce | flops 2048 | bytes 16384 | tf_op jit(solution)/shard_map/psum | solution.py:69
  630.6 3.5 reshape.104
  634.1 5.1 reduce.2
  639.1 2.1 broadcast_in_dim_reshape.3
  641.2 2.7 fusion.43
  643.9 2.1 fusion.42
  (14 shorter events, 0.1 us)
Async XLA Ops:
  7.2 329.4 %copy-start = (bf16[1,2048,768]{2,1,0:T(8,128)(2,1)S(1)}, bf16[1,2048,768]{2,1,0:T(8,128)(2,1)}, u32[]{:S(2)}) copy-start(bf16[1,2048,768]{2,1,0:T(8,128)(2,1)} %param.12) | copy-start | bytes 9437188
  22.1 88.0 %all-to-all-start = ((bf16[16,2,8192]{2,1,0:T(2,128)(2,1)}), bf16[16,2,8192]{2,1,0:T(2,128)(2,1)}, u32[]{:S(2)}, u32[]{:S(2)}) async-start(bf16[16,2,8192]{2,1,0:T(2,128)(2,1)} %reshape.97), calls=%async_computation | async-start | bytes 1048576 | tf_op jit(solution)/shard_map/all_to_all | solution.py:36
  53.5 45.1 %collective-permute-start = (bf16[1,128,2048]{2,1,0:T(8,128)(2,1)}, bf16[1,128,2048]{2,1,0:T(8,128)(2,1)}, u32[]{:S(2)}, u32[]{:S(2)}) collective-permute-start(bf16[1,128,2048]{2,1,0:T(8,128)(2,1)} %param.7), channel_id=1, source_target_pairs={{960,0},{0,64},{64,128},{128,192},{192,256},{256,320},{320,384},{3... | collective-permute-start | bytes 1572872 | tf_op jit(solution)/shard_map/ppermute | solution.py:12
  110.1 107.2 %all-to-all-start.2 = ((bf16[16,2,8192]{2,1,0:T(2,128)(2,1)}), bf16[16,2,8192]{2,1,0:T(2,128)(2,1)}, u32[]{:S(2)}, u32[]{:S(2)}) async-start(bf16[16,2,8192]{2,1,0:T(2,128)(2,1)} %reshape.101), calls=%async_computation.2 | async-start | bytes 1048576 | tf_op jit(solution)/shard_map/all_to_all | solution.py:35
  217.3 81.6 %all-to-all-start.1 = ((bf16[16,2,8192]{2,1,0:T(2,128)(2,1)}), bf16[16,2,8192]{2,1,0:T(2,128)(2,1)}, u32[]{:S(2)}, u32[]{:S(2)}) async-start(bf16[16,2,8192]{2,1,0:T(2,128)(2,1)} %reshape.99), calls=%async_computation.1 | async-start | bytes 1048576 | tf_op jit(solution)/shard_map/all_to_all | solution.py:40
  235.9 99.4 %copy-start.1 = (f32[1,2048]{1,0:T(1,128)S(1)}, f32[1,2048]{1,0:T(1,128)}, u32[]{:S(2)}) copy-start(f32[1,2048]{1,0:T(1,128)} %param.11) | copy-start | bytes 24580
  298.9 331.7 %all-to-all-start.3 = ((bf16[16,2,8192]{2,1,0:T(2,128)(2,1)}), bf16[16,2,8192]{2,1,0:T(2,128)(2,1)}, u32[]{:S(2)}, u32[]{:S(2)}) async-start(bf16[16,2,8192]{2,1,0:T(2,128)(2,1)} %reshape.103), calls=%async_computation.3 | async-start | bytes 1048576 | tf_op jit(solution)/shard_map/all_to_all | solution.py:39
  323.0 271.2 %all-reduce.3.cloned.1.call-start = ((), (), s32[]{:S(2)}) async-start(), calls=%async_computation.4 | async-start | bytes 2097152 | tf_op jit(solution)/shard_map/psum | solution.py:60
  323.0 69.1 %collective-permute-start.1 = (bf16[1,128,2048]{2,1,0:T(8,128)(2,1)}, bf16[1,128,2048]{2,1,0:T(8,128)(2,1)}, u32[]{:S(2)}, u32[]{:S(2)}) collective-permute-start(bf16[1,128,2048]{2,1,0:T(8,128)(2,1)} %param.8), channel_id=1, source_target_pairs={{64,0},{128,64},{192,128},{256,192},{320,256},{384,320},{448,384},... | collective-permute-start | bytes 1572872 | tf_op jit(solution)/shard_map/ppermute | solution.py:12
Sparse Core Ops, SparseCore 0:
  397.4 196.6 all-reduce.2
where the time goes:
time: 661 us; the launch traced here: 653 us
  waiting for transfers between devices  280 us (42%)
  local copies, waits for them, and re-layouts  160 us (24%)
  starting transfers between devices  110 us (17%)
  other arithmetic  42.1 us (6%)
  blocking collectives  34.6 us (5%)
  between operations  14.9 us (2%)
  matrix products  11 us (2%)
    psum x1, waiting for transfers between devices, body(): lax.psum(mixed_part.astype(jnp.bfloat16), 'tensor').astype(jnp.float32)  197 us
    ppermute x2, waiting for transfers between devices, shifted(): return lax.ppermute(block, axis, route)  57.7 us
    rev x1, local copies, waits for them, and re-layouts, body(): spread_first[::-1]  55.4 us
    rev x1, local copies, waits for them, and re-layouts, body(): spread_second[::-1]  55.4 us
    psum x1, blocking collectives, body(): gain_total = lax.psum(jnp.sum(normed_grad * saved_hat, axis=0), 'dp')  34.6 us
    all_to_all x1, starting transfers between devices, body(): lax.all_to_all(second_flat, 'pipe', split_axis=0, concat_axis=0, tiled=True)  31.3 us
    unnamed x16, local copies, waits for them, and re-layouts  28.1 us
    all_to_all x1, waiting for transfers between devices, body(): lax.all_to_all(first_flat, 'pipe', split_axis=0, concat_axis=0, tiled=True)  25.9 us
  transfers between devices with their start and end apart: 7, of which 4 were waited for; matrix products, arithmetic and copies ran while one was open for 28% of the time, Pallas kernels for 0%

commit v1 on v0

v1 whole, which is shorter than its diff:
```python
import functools

import jax
import jax.numpy as jnp
from jax import lax
from jax.experimental import pallas as pl
from jax.experimental.pallas import tpu as pltpu
from jax.sharding import PartitionSpec as P

epsilon = 1e-05
MESH = pl.DeviceIdType.MESH
F32, BF16 = jnp.float32, jnp.bfloat16
TILE = 256


def remote(src, dst, send, recv, **where):
    return pltpu.make_async_remote_copy(
        src_ref=src, dst_ref=dst, send_sem=send, recv_sem=recv, device_id=where, device_id_type=MESH
    )


def rms(values):
    factor = lax.rsqrt(jnp.mean(values * values, axis=-1, keepdims=True) + epsilon)
    return values * factor, factor


def kernel(
    n_pipe, n_dp, n_tensor,
    slot_ref, out_in, grad_in, host_in, gain_ref, up_in, down_in,
    nf_out, nb_out, th_out, gg_out,
    up, down, both, chosen, fwd_own, sav_own, hat_own,
    norm_f, norm_s, inc, part_f, part_b, sum_f, sum_b, end_f, end_b,
    mid, gain_own, gain_dp, gain_mid, gain_tp,
    local_sem, z_send, z_recv, ag_send, ag_recv, rs_send, rs_recv, gd_send, gd_recv, gt_send, gt_recv,
):
    s, d, t = lax.axis_index("pipe"), lax.axis_index("dp"), lax.axis_index("tensor")
    rows = out_in.shape[1] // n_tensor
    width, hidden_units = up.shape
    core = t % 2
    sibling = t + 1 - 2 * core
    across = [(t + 2 * p) % n_tensor for p in range(1, n_tensor // 2)]
    peers = [(t + p) % n_tensor for p in range(1, n_tensor)]
    dp_peers = [(d + p) % n_dp for p in range(1, n_dp)]
    after, before = (s + 1) % n_pipe, (s + n_pipe - 1) % n_pipe
    mirror, keeper = n_pipe - 1 - s, (2 * n_pipe - 2 - s) % n_pipe
    own = pl.ds(pl.multiple_of(t * rows, rows), rows)

    def chunk(ref, k):
        return ref.at[0, pl.ds(pl.multiple_of(k * rows, rows), rows)]

    load_host = pltpu.make_async_copy(host_in.at[0, :, own], both, local_sem.at[0])
    load_host.start()
    load_up = pltpu.make_async_copy(up_in.at[0], up, local_sem.at[1])
    load_up.start()
    load_down = pltpu.make_async_copy(down_in.at[0], down, local_sem.at[2])
    load_down.start()

    barrier = pltpu.get_barrier_semaphore()
    for where in [{"pipe": after}, {"pipe": before}, {"pipe": mirror}]:
        pl.semaphore_signal(barrier, inc=1, device_id=where, device_id_type=MESH)

    @pl.when(keeper != s)
    def _():
        pl.semaphore_signal(barrier, inc=1, device_id={"pipe": keeper}, device_id_type=MESH)

    for k in dp_peers:
        pl.semaphore_signal(barrier, inc=1, device_id={"dp": k}, device_id_type=MESH)
    for k in peers:
        pl.semaphore_signal(barrier, inc=1, device_id={"tensor": k}, device_id_type=MESH)
    load_host.wait()
    chosen[...] = both[slot_ref[0]]
    pl.semaphore_wait(barrier, 3 + len(dp_peers) + len(peers) + jnp.where(keeper != s, 1, 0))

    z_s = remote(chosen, sav_own, z_send.at[0], z_recv.at[0], pipe=mirror)
    z_g = remote(grad_in.at[0, own], inc.at[t], z_send.at[1], z_recv.at[1], pipe=before)
    z_f = remote(out_in.at[0, own], fwd_own, z_send.at[2], z_recv.at[2], pipe=after)
    z_t = remote(out_in.at[0, own], chunk(th_out, t), z_send.at[3], z_recv.at[3], pipe=keeper)
    l_t = pltpu.make_async_copy(out_in.at[0, own], chunk(th_out, t), local_sem.at[3])
    z_s.start()
    z_g.start()
    z_f.start()

    def gather_start(which, at):
        for i, k in enumerate([sibling] + across):
            remote(at(t), at(t), ag_send.at[which, i], ag_recv.at[which, t], tensor=k).start()

    def gather_pass(which, at):
        for i, k in enumerate(across):
            remote(at(k), at(k), ag_send.at[which, 4 + i], ag_recv.at[which, k], tensor=k).wait_recv()
            remote(at(k), at(k), ag_send.at[which, 4 + i], ag_recv.at[which, k], tensor=sibling).start()

    def gather_wait(which, at):
        for k in [sibling] + [k + 1 - 2 * core for k in across]:
            remote(at(k), at(k), ag_send.at[which, 0], ag_recv.at[which, k], tensor=sibling).wait_recv()

    def gather_sent(which, at):
        for i, k in enumerate([sibling] + across):
            remote(at(t), at(t), ag_send.at[which, i], ag_recv.at[which, t], tensor=k).wait_send()
        for i, k in enumerate(across):
            remote(at(k), at(k), ag_send.at[which, 4 + i], ag_recv.at[which, k], tensor=sibling).wait_send()

    at_s, at_g, at_f = (lambda k: norm_s.at[k]), (lambda k: inc.at[k]), (lambda k: norm_f.at[k])
    at_t, at_nb, at_nf = (
        functools.partial(chunk, th_out), functools.partial(chunk, nb_out), functools.partial(chunk, nf_out)
    )
    gains = gain_ref[...]

    z_s.wait_recv()
    hat, saved_factor = rms(sav_own[...].astype(F32))
    hat_own[...] = hat
    norm_s[t] = (hat * gains).astype(BF16)
    gather_start(0, at_s)
    z_g.wait_recv()
    gather_start(1, at_g)
    z_f.wait_recv()
    norm_f[t] = (rms(fwd_own[...].astype(F32))[0] * gains).astype(BF16)
    gather_start(2, at_f)

    @pl.when(keeper != s)
    def _():
        z_t.start()

    @pl.when(keeper == s)
    def _():
        l_t.start()

    gather_pass(0, at_s)
    gather_pass(1, at_g)
    gather_pass(2, at_f)
    gather_wait(0, at_s)
    gather_wait(1, at_g)

    tokens = n_tensor * rows
    nt = (((1,), (1,)), ((), ()))

    def cut(i):
        return pl.ds(pl.multiple_of(i * TILE, TILE), TILE)

    load_up.wait()
    load_down.wait()

    @pl.loop(0, hidden_units // TILE)
    def _(i):
        pre = jnp.dot(norm_s[...].reshape(tokens, width), up[:, cut(i)], preferred_element_type=F32)
        back = lax.dot_general(inc[...].reshape(tokens, width), down[cut(i), :], nt, preferred_element_type=F32)
        sigma = jax.nn.sigmoid(pre)
        mid[0, :, cut(i)] = (back * (sigma * (1.0 + pre * (1.0 - sigma)))).astype(BF16)

    @pl.loop(0, width // TILE)
    def _(i):
        part = lax.dot_general(mid[0], up[cut(i), :], nt, preferred_element_type=F32)
        part_b[:, :, cut(i)] = part.astype(BF16).reshape(n_tensor, rows, TILE)

    def scatter_start(which, part, total):
        for i, k in enumerate(peers):
            remote(part.at[k], total.at[t], rs_send.at[which, i], rs_recv.at[which, t], tensor=k).start()

    def scatter_sum(which, part, total):
        acc = part[t].astype(F32)
        for i, k in enumerate(peers):
            remote(part.at[k], total.at[k], rs_send.at[which, i], rs_recv.at[which, k], tensor=k).wait_recv()
            acc += total[k].astype(F32)
        return acc

    def scatter_sent(which, part, total):
        for i, k in enumerate(peers):
            remote(part.at[k], total.at[t], rs_send.at[which, i], rs_recv.at[which, t], tensor=k).wait_send()

    scatter_start(0, part_b, sum_b)
    gather_wait(2, at_f)

    @pl.loop(0, hidden_units // TILE)
    def _(i):
        pre = jnp.dot(norm_f[...].reshape(tokens, width), up[:, cut(i)], preferred_element_type=F32)
        mid[1, :, cut(i)] = jax.nn.silu(pre).astype(BF16)

    @pl.loop(0, width // TILE)
    def _(i):
        part = jnp.dot(mid[1], down[:, cut(i)], preferred_element_type=F32)
        part_f[:, :, cut(i)] = part.astype(BF16).reshape(n_tensor, rows, TILE)

    scatter_start(1, part_f, sum_f)

    normed_grad = scatter_sum(0, part_b, sum_b)
    hat = hat_own[...]
    gain_own[...] = jnp.sum(normed_grad * hat, axis=0, keepdims=True)
    for i, k in enumerate(dp_peers):
        remote(gain_own, gain_dp.at[d], gd_send.at[i], gd_recv.at[d], dp=k).start()
    hat_grad = normed_grad * gains
    input_grad = saved_factor * (hat_grad - hat * jnp.mean(hat_grad * hat, axis=-1, keepdims=True))
    end_b[...] = (inc[t].astype(F32) + input_grad).astype(BF16)

    def ends_start(which, end, at):
        keep = pltpu.make_async_copy(end, at(t), local_sem.at[which])
        keep.start()
        for i, k in enumerate([sibling] + across):
            remote(end, at(t), ag_send.at[which, i], ag_recv.at[which, t], tensor=k).start()
        return keep

    keep_b = ends_start(4, end_b, at_nb)
    mixed = scatter_sum(1, part_f, sum_f)
    end_f[...] = (fwd_own[...].astype(F32) + mixed).astype(BF16)
    keep_f = ends_start(5, end_f, at_nf)

    @pl.when(keeper != s)
    def _():
        z_t.wait()

    @pl.when(keeper == s)
    def _():
        l_t.wait()

    gather_start(3, at_t)

    acc = gain_own[...]
    for i, k in enumerate(dp_peers):
        remote(gain_own, gain_dp.at[k], gd_send.at[i], gd_recv.at[k], dp=k).wait_recv()
        acc += gain_dp[k]
    gain_mid[...] = acc
    for i, k in enumerate(peers):
        remote(gain_mid, gain_tp.at[t], gt_send.at[i], gt_recv.at[t], tensor=k).start()

    gather_pass(4, at_nb)
    gather_pass(5, at_nf)
    gather_pass(3, at_t)

    for i, k in enumerate(peers):
        remote(gain_mid, gain_tp.at[k], gt_send.at[i], gt_recv.at[k], tensor=k).wait_recv()
        acc += gain_tp[k]
    gg_out[...] = acc

    gather_wait(4, at_nb)
    gather_wait(5, at_nf)
    gather_wait(3, at_t)
    keep_b.wait()
    keep_f.wait()
    z_s.wait_send()
    z_g.wait_send()
    z_f.wait_send()
    for which, at in enumerate((at_s, at_g, at_f, at_t, at_nb, at_nf)):
        gather_sent(which, at)
    scatter_sent(0, part_b, sum_b)
    scatter_sent(1, part_f, sum_f)
    for i, k in enumerate(dp_peers):
        remote(gain_own, gain_dp.at[d], gd_send.at[i], gd_recv.at[d], dp=k).wait_send()
    for i, k in enumerate(peers):
        remote(gain_mid, gain_tp.at[t], gt_send.at[i], gt_recv.at[t], tensor=k).wait_send()


def body(section_out, section_grad, hosted, send_slot, gain, w_up, w_down):
    n_pipe, n_dp, n_tensor = (lax.axis_size(a) for a in ("pipe", "dp", "tensor"))
    _, tokens, width = section_out.shape
    units = w_up.shape[2]
    rows = tokens // n_tensor
    dma = pltpu.SemaphoreType.DMA
    whole = jax.ShapeDtypeStruct(section_out.shape, BF16)
    anywhere = pl.BlockSpec(memory_space=pl.ANY)
    in_vmem = pl.BlockSpec(memory_space=pltpu.VMEM)
    gathered = pltpu.VMEM((n_tensor, rows, width), BF16)
    row_block = pltpu.VMEM((rows, width), BF16)
    gain_row = pltpu.VMEM((1, width), F32)
    return pl.pallas_call(
        functools.partial(kernel, n_pipe, n_dp, n_tensor),
        out_shape=(whole, whole, whole, jax.ShapeDtypeStruct((1, width), F32)),
        in_specs=[
            pl.BlockSpec(memory_space=pltpu.SMEM), anywhere, anywhere, anywhere, in_vmem, anywhere, anywhere,
        ],
        out_specs=(anywhere, anywhere, anywhere, in_vmem),
        scratch_shapes=[
            pltpu.VMEM((width, units), BF16), pltpu.VMEM((units, width), BF16),
            pltpu.VMEM((hosted.shape[1], rows, width), BF16), row_block, row_block, row_block,
            pltpu.VMEM((rows, width), F32),
            gathered, gathered, gathered, gathered, gathered, gathered, gathered, row_block, row_block,
            pltpu.VMEM((2, tokens, units), BF16),
            gain_row, pltpu.VMEM((n_dp, 1, width), F32), gain_row, pltpu.VMEM((n_tensor, 1, width), F32),
            dma((6,)), dma((4,)), dma((4,)), dma((6, n_tensor)), dma((6, n_tensor)),
            dma((2, n_tensor)), dma((2, n_tensor)), dma((n_dp,)), dma((n_dp,)), dma((n_tensor,)), dma((n_tensor,)),
        ],
        compiler_params=pltpu.CompilerParams(
            collective_id=0, has_side_effects=True, vmem_limit_bytes=50 * 2**20
        ),
    )(send_slot, section_out, section_grad, hosted, gain, w_up, w_down)


def solution(mesh):
    placed = (
        P("pipe", "dp", None),
        P("pipe", "dp", None),
        P("pipe", None, "dp", None),
        P("pipe"),
        P("pipe", None),
        P("pipe", None, "tensor"),
        P("pipe", "tensor", None),
    )
    return jax.shard_map(
        body,
        mesh=mesh,
        in_specs=placed,
        out_specs=(
            P("pipe", "dp", None),
            P("pipe", "dp", None),
            P("pipe", "dp", None),
            P("pipe", None),
        ),
        check_vma=False,
    )
```

time: 661 us -> 95.8 us (0.14)
  the two profiles are of different devices: /device:TPU:2 before, /device:TPU:1 now
where the time goes in v1:
time: 95.8 us; the launch traced here: 94.8 us
  Pallas kernels  86.5 us (90%)
  local copies, waits for them, and re-layouts  6.98 us (7%)
  between operations  1.3 us (1%)
    pallas_call x1, Pallas kernels, body(): pl.pallas_call(functools.partial(kernel, n_pipe, n_dp, n_tensor), out_sha...  86.5 us
    unnamed x12, local copies, waits for them, and re-layouts  6.98 us

profile of v1, /device:TPU:1, one launch (start us, length us, event | category | flops | bytes accessed | tf_op | source)
XLA Modules:
  0.0 94.8 jit_solution(16534314752410779273)
XLA Ops:
  1.3 0.0 copy-start
  1.3 1.2 %copy-done = bf16[1,2,128,2048]{3,2,1,0:T(8,128)(2,1)S(1)} copy-done((bf16[1,2,128,2048]{3,2,1,0:T(8,128)(2,1)S(1)}, bf16[1,2,128,2048]{3,2,1,0:T(8,128)(2,1)}, u32[]{:S(2)}) %copy-start) | copy-done | bytes 1048600
  2.5 0.0 copy-start.1
  2.5 1.0 %copy-done.1 = bf16[1,128,2048]{2,1,0:T(8,128)(2,1)S(1)} copy-done((bf16[1,128,2048]{2,1,0:T(8,128)(2,1)S(1)}, bf16[1,128,2048]{2,1,0:T(8,128)(2,1)}, u32[]{:S(2)}) %copy-start.1) | copy-done | bytes 524312
  3.5 0.0 copy-start.2
  3.5 1.0 %copy-done.2 = bf16[1,128,2048]{2,1,0:T(8,128)(2,1)S(1)} copy-done((bf16[1,128,2048]{2,1,0:T(8,128)(2,1)S(1)}, bf16[1,128,2048]{2,1,0:T(8,128)(2,1)}, u32[]{:S(2)}) %copy-start.2) | copy-done | bytes 524312
  4.6 0.0 copy-start.3
  4.6 0.7 copy-done.3
  5.3 86.5 %shard_map.102 = (bf16[1,128,2048]{2,1,0:T(8,128)(2,1)S(1)}, bf16[1,128,2048]{2,1,0:T(8,128)(2,1)S(1)}, bf16[1,128,2048]{2,1,0:T(8,128)(2,1)S(1)}, f32[1,2048]{1,0:T(1,128)S(1)}) custom-call(s32[1]{0:T(128)S(6)} %copy.15.slot_ref, bf16[1,128,2048]{2,1,0:T(8,128)(2,1)S(1)} %copy-done.1, bf16[1,128,2048]{2,1,0:T(8,128)(2,1)S(1)} %copy-done.2, ...), custom_call_target="tpu_custom_call" | custom-call | tf_op jit(solution)/shard_map/pallas_call | solution.py:262
  91.8 0.8 copy.16
  92.6 0.8 copy.17
  93.4 0.8 copy.18
  94.2 0.6 copy.19
Async XLA Ops:
  1.3 1.2 %copy-start = (bf16[1,2,128,2048]{3,2,1,0:T(8,128)(2,1)S(1)}, bf16[1,2,128,2048]{3,2,1,0:T(8,128)(2,1)}, u32[]{:S(2)}) copy-start(bf16[1,2,128,2048]{3,2,1,0:T(8,128)(2,1)} %host_in.1) | copy-start | bytes 3145732
  2.5 1.0 %copy-start.1 = (bf16[1,128,2048]{2,1,0:T(8,128)(2,1)S(1)}, bf16[1,128,2048]{2,1,0:T(8,128)(2,1)}, u32[]{:S(2)}) copy-start(bf16[1,128,2048]{2,1,0:T(8,128)(2,1)} %out_in.1) | copy-start | bytes 1572868
  3.5 1.0 %copy-start.2 = (bf16[1,128,2048]{2,1,0:T(8,128)(2,1)S(1)}, bf16[1,128,2048]{2,1,0:T(8,128)(2,1)}, u32[]{:S(2)}) copy-start(bf16[1,128,2048]{2,1,0:T(8,128)(2,1)} %grad_in.1) | copy-start | bytes 1572868
  4.6 0.7 copy-start.3

commit v2 on v1

--- a/solution.py
+++ b/solution.py
@@ -11,6 +11,7 @@
 MESH = pl.DeviceIdType.MESH
 F32, BF16 = jnp.float32, jnp.bfloat16
 TILE = 256
+CUTS = 4
 
 
 def remote(src, dst, send, recv, **where):
@@ -30,8 +31,8 @@
     nf_out, nb_out, th_out, gg_out,
     up, down, both, chosen, fwd_own, sav_own, hat_own,
     norm_f, norm_s, inc, part_f, part_b, sum_f, sum_b, end_f, end_b,
-    mid, gain_own, gain_dp, gain_mid, gain_tp,
-    local_sem, z_send, z_recv, ag_send, ag_recv, rs_send, rs_recv, gd_send, gd_recv, gt_send, gt_recv,
+    mid, pair, gain_own, gain_dp, gain_mid, gain_tp,
+    local_sem, z_send, z_recv, ag_send, ag_recv, rs_send, rs_recv, pr_send, pr_recv, gd_send, gd_recv, gt_send, gt_recv,
 ):
     s, d, t = lax.axis_index("pipe"), lax.axis_index("dp"), lax.axis_index("tensor")
     rows = out_in.shape[1] // n_tensor
@@ -151,20 +152,39 @@
         part = lax.dot_general(mid[0], up[cut(i), :], nt, preferred_element_type=F32)
         part_b[:, :, cut(i)] = part.astype(BF16).reshape(n_tensor, rows, TILE)
 
+    y_own, y_all = t // 2, n_tensor // 2
+    far = [(y_own + p) % y_all for p in sorted(range(1, y_all), key=lambda p: -min(p, y_all - p))]
+
+    def pair_copy(which, part, y):
+        k = 2 * y + 1 - core
+        return remote(part.at[k], pair.at[which, y], pr_send.at[which, y], pr_recv.at[which, y], tensor=sibling)
+
+    def pair_sum(which, part, y):
+        pair_copy(which, part, y).wait_recv()
+        return part[2 * y + core].astype(F32) + pair[which, y].astype(F32)
+
     def scatter_start(which, part, total):
-        for i, k in enumerate(peers):
-            remote(part.at[k], total.at[t], rs_send.at[which, i], rs_recv.at[which, t], tensor=k).start()
+        for y in far + [y_own]:
+            pair_copy(which, part, y).start()
+        for i, y in enumerate(far):
+            k = 2 * y + core
+            part[k] = pair_sum(which, part, y).astype(BF16)
+            remote(part.at[k], total.at[y_own], rs_send.at[which, i], rs_recv.at[which, y_own], tensor=k).start()
 
     def scatter_sum(which, part, total):
-        acc = part[t].astype(F32)
-        for i, k in enumerate(peers):
-            remote(part.at[k], total.at[k], rs_send.at[which, i], rs_recv.at[which, k], tensor=k).wait_recv()
-            acc += total[k].astype(F32)
+        acc = pair_sum(which, part, y_own)
+        for i, y in enumerate(far):
+            k = 2 * y + core
+            remote(part.at[k], total.at[y], rs_send.at[which, i], rs_recv.at[which, y], tensor=k).wait_recv()
+            acc += total[y].astype(F32)
         return acc
 
     def scatter_sent(which, part, total):
-        for i, k in enumerate(peers):
-            remote(part.at[k], total.at[t], rs_send.at[which, i], rs_recv.at[which, t], tensor=k).wait_send()
+        for y in far + [y_own]:
+            pair_copy(which, part, y).wait_send()
+        for i, y in enumerate(far):
+            k = 2 * y + core
+            remote(part.at[k], total.at[y_own], rs_send.at[which, i], rs_recv.at[which, y_own], tensor=k).wait_send()
 
     scatter_start(0, part_b, sum_b)
     gather_wait(2, at_f)
@@ -247,6 +267,23 @@
         remote(gain_mid, gain_tp.at[t], gt_send.at[i], gt_recv.at[t], tensor=k).wait_send()
 
 
+def move_out(*refs):
+    sources, ends, held, gain_held, sems, gain_sem = refs[:4], refs[4:8], *refs[8:]
+    rows = sources[0].shape[1] // CUTS
+    steps = [(sources[3], gain_held, ends[3], gain_sem)]
+    for i in range(3):
+        for j in range(CUTS):
+            part = pl.ds(j * rows, rows)
+            steps.append((sources[i].at[0, part], held.at[i, part], ends[i].at[0, part], sems.at[i, j]))
+    for source, spot, _, sem in steps:
+        pltpu.make_async_copy(source, spot, sem).start()
+    for source, spot, end, sem in steps:
+        pltpu.make_async_copy(source, spot, sem).wait()
+        pltpu.make_async_copy(spot, end, sem).start()
+    for _, spot, end, sem in steps:
+        pltpu.make_async_copy(spot, end, sem).wait()
+
+
 def body(section_out, section_grad, hosted, send_slot, gain, w_up, w_down):
     n_pipe, n_dp, n_tensor = (lax.axis_size(a) for a in ("pipe", "dp", "tensor"))
     _, tokens, width = section_out.shape
@@ -259,7 +296,7 @@
     gathered = pltpu.VMEM((n_tensor, rows, width), BF16)
     row_block = pltpu.VMEM((rows, width), BF16)
     gain_row = pltpu.VMEM((1, width), F32)
-    return pl.pallas_call(
+    results = pl.pallas_call(
         functools.partial(kernel, n_pipe, n_dp, n_tensor),
         out_shape=(whole, whole, whole, jax.ShapeDtypeStruct((1, width), F32)),
         in_specs=[
@@ -271,15 +308,23 @@
             pltpu.VMEM((hosted.shape[1], rows, width), BF16), row_block, row_block, row_block,
             pltpu.VMEM((rows, width), F32),
             gathered, gathered, gathered, gathered, gathered, gathered, gathered, row_block, row_block,
-            pltpu.VMEM((2, tokens, units), BF16),
+            pltpu.VMEM((2, tokens, units), BF16), pltpu.VMEM((2, n_tensor // 2, rows, width), BF16),
             gain_row, pltpu.VMEM((n_dp, 1, width), F32), gain_row, pltpu.VMEM((n_tensor, 1, width), F32),
             dma((6,)), dma((4,)), dma((4,)), dma((6, n_tensor)), dma((6, n_tensor)),
-            dma((2, n_tensor)), dma((2, n_tensor)), dma((n_dp,)), dma((n_dp,)), dma((n_tensor,)), dma((n_tensor,)),
+            dma((2, n_tensor)), dma((2, n_tensor)), dma((2, n_tensor)), dma((2, n_tensor)), dma((n_dp,)), dma((n_dp,)), dma((n_tensor,)), dma((n_tensor,)),
         ],
         compiler_params=pltpu.CompilerParams(
-            collective_id=0, has_side_effects=True, vmem_limit_bytes=50 * 2**20
+            collective_id=0, has_side_effects=True, vmem_limit_bytes=60 * 2**20
         ),
     )(send_slot, section_out, section_grad, hosted, gain, w_up, w_down)
+    return pl.pallas_call(
+        move_out,
+        out_shape=tuple(jax.ShapeDtypeStruct(r.shape, r.dtype) for r in results),
+        in_specs=[anywhere] * 4,
+        out_specs=(anywhere,) * 4,
+        scratch_shapes=[pltpu.VMEM((3, tokens, width), BF16), gain_row, dma((3, CUTS)), dma(())],
+        compiler_params=pltpu.CompilerParams(vmem_limit_bytes=60 * 2**20),
+    )(*results)
 
 
 def solution(mesh):

time: 95.8 us -> 90 us (0.939)
  local copies, waits for them, and re-layouts: 6.98 us -> 0 us
  Pallas kernels: 86.5 us -> 88.5 us
    unnamed x12 -> x0, local copies, waits for them, and re-layouts: 6.98 us -> none
    pallas_call x0 -> x1, Pallas kernels: none -> 2.46 us  [body(): pl.pallas_call(move_out, out_shape=tuple((jax.ShapeDtypeStruct(r.shape, r...]
where the time goes in v2:
time: 90 us; the launch traced here: 89.8 us
  Pallas kernels  88.5 us (98%)
  between operations  1.29 us (1%)
    pallas_call x1, Pallas kernels, body(): pl.pallas_call(functools.partial(kernel, n_pipe, n_dp, n_tensor), out_sha...  86 us
    pallas_call x1, Pallas kernels, body(): pl.pallas_call(move_out, out_shape=tuple((jax.ShapeDtypeStruct(r.shape, r...  2.46 us

profile of v2, /device:TPU:1, one launch (start us, length us, event | category | flops | bytes accessed | tf_op | source)
XLA Modules:
  0.0 89.8 jit_solution(15686189139756032773)
XLA Ops:
  1.3 86.0 %shard_map.102 = (bf16[1,128,2048]{2,1,0:T(8,128)(2,1)}, bf16[1,128,2048]{2,1,0:T(8,128)(2,1)}, bf16[1,128,2048]{2,1,0:T(8,128)(2,1)}, f32[1,2048]{1,0:T(1,128)}) custom-call(s32[1]{0:T(128)S(6)} %copy.11.slot_ref, bf16[1,128,2048]{2,1,0:T(8,128)(2,1)} %out_in.1, bf16[1,128,2048]{2,1,0:T(8,128)(2,1)} %grad_in.1, bf16[1,2,128,2048]{3,2,1,0:T(8,128)(2,1)} %host_in.1, ...), custom_call_target="tpu_custom_call" | custom-call | tf_op jit(solution)/shard_map/pallas_call | solution.py:299
  87.3 2.5 %shard_map.103 = (bf16[1,128,2048]{2,1,0:T(8,128)(2,1)}, bf16[1,128,2048]{2,1,0:T(8,128)(2,1)}, bf16[1,128,2048]{2,1,0:T(8,128)(2,1)}, f32[1,2048]{1,0:T(1,128)}) custom-call(bf16[1,128,2048]{2,1,0:T(8,128)(2,1)} %get-tuple-element.8.refs_0_, bf16[1,128,2048]{2,1,0:T(8,128)(2,1)} %get-tuple-element.9.refs_1_, ...), custom_call_target="tpu_custom_call" | custom-call | tf_op jit(solution)/shard_map/pallas_call | solution.py:320

commit v3 on v2

--- a/solution.py
+++ b/solution.py
@@ -49,25 +49,25 @@
     def chunk(ref, k):
         return ref.at[0, pl.ds(pl.multiple_of(k * rows, rows), rows)]
 
+    barrier = pltpu.get_barrier_semaphore()
+    @pl.when(keeper != s)
+    def _():
+        pl.semaphore_signal(barrier, inc=1, device_id={"pipe": keeper}, device_id_type=MESH)
+
+    for where in [{"pipe": after}, {"pipe": before}, {"pipe": mirror}]:
+        pl.semaphore_signal(barrier, inc=1, device_id=where, device_id_type=MESH)
+
+    for k in dp_peers:
+        pl.semaphore_signal(barrier, inc=1, device_id={"dp": k}, device_id_type=MESH)
+    for k in peers:
+        pl.semaphore_signal(barrier, inc=1, device_id={"tensor": k}, device_id_type=MESH)
+
     load_host = pltpu.make_async_copy(host_in.at[0, :, own], both, local_sem.at[0])
     load_host.start()
     load_up = pltpu.make_async_copy(up_in.at[0], up, local_sem.at[1])
     load_up.start()
     load_down = pltpu.make_async_copy(down_in.at[0], down, local_sem.at[2])
     load_down.start()
-
-    barrier = pltpu.get_barrier_semaphore()
-    for where in [{"pipe": after}, {"pipe": before}, {"pipe": mirror}]:
-        pl.semaphore_signal(barrier, inc=1, device_id=where, device_id_type=MESH)
-
-    @pl.when(keeper != s)
-    def _():
-        pl.semaphore_signal(barrier, inc=1, device_id={"pipe": keeper}, device_id_type=MESH)
-
-    for k in dp_peers:
-        pl.semaphore_signal(barrier, inc=1, device_id={"dp": k}, device_id_type=MESH)
-    for k in peers:
-        pl.semaphore_signal(barrier, inc=1, device_id={"tensor": k}, device_id_type=MESH)
     load_host.wait()
     chosen[...] = both[slot_ref[0]]
     pl.semaphore_wait(barrier, 3 + len(dp_peers) + len(peers) + jnp.where(keeper != s, 1, 0))
@@ -268,20 +268,17 @@
 
 
 def move_out(*refs):
-    sources, ends, held, gain_held, sems, gain_sem = refs[:4], refs[4:8], *refs[8:]
+    sources, ends, (sems, gain_sem) = refs[:4], refs[4:8], refs[8:]
+    copies = [pltpu.make_async_copy(sources[3], ends[3], gain_sem)]
     rows = sources[0].shape[1] // CUTS
-    steps = [(sources[3], gain_held, ends[3], gain_sem)]
     for i in range(3):
         for j in range(CUTS):
             part = pl.ds(j * rows, rows)
-            steps.append((sources[i].at[0, part], held.at[i, part], ends[i].at[0, part], sems.at[i, j]))
-    for source, spot, _, sem in steps:
-        pltpu.make_async_copy(source, spot, sem).start()
-    for source, spot, end, sem in steps:
-        pltpu.make_async_copy(source, spot, sem).wait()
-        pltpu.make_async_copy(spot, end, sem).start()
-    for _, spot, end, sem in steps:
-        pltpu.make_async_copy(spot, end, sem).wait()
+            copies.append(pltpu.make_async_copy(sources[i].at[0, part], ends[i].at[0, part], sems.at[i, j]))
+    for copy in copies:
+        copy.start()
+    for copy in copies:
+        copy.wait()
 
 
 def body(section_out, section_grad, hosted, send_slot, gain, w_up, w_down):
@@ -314,7 +311,7 @@
             dma((2, n_tensor)), dma((2, n_tensor)), dma((2, n_tensor)), dma((2, n_tensor)), dma((n_dp,)), dma((n_dp,)), dma((n_tensor,)), dma((n_tensor,)),
         ],
         compiler_params=pltpu.CompilerParams(
-            collective_id=0, has_side_effects=True, vmem_limit_bytes=60 * 2**20
+            collective_id=0, has_side_effects=True, vmem_limit_bytes=52 * 2**20
         ),
     )(send_slot, section_out, section_grad, hosted, gain, w_up, w_down)
     return pl.pallas_call(
@@ -322,8 +319,8 @@
         out_shape=tuple(jax.ShapeDtypeStruct(r.shape, r.dtype) for r in results),
         in_specs=[anywhere] * 4,
         out_specs=(anywhere,) * 4,
-        scratch_shapes=[pltpu.VMEM((3, tokens, width), BF16), gain_row, dma((3, CUTS)), dma(())],
-        compiler_params=pltpu.CompilerParams(vmem_limit_bytes=60 * 2**20),
+        scratch_shapes=[dma((3, CUTS)), dma(())],
+        compiler_params=pltpu.CompilerParams(vmem_limit_bytes=16 * 2**20),
     )(*results)
 
 

time: 90 us -> 88.2 us (0.980)
  Pallas kernels: 88.5 us -> 86.1 us
    pallas_call x1, Pallas kernels: 2.46 us -> 1.25 us  [body(): pl.pallas_call(move_out, out_shape=tuple((jax.ShapeDtypeStruct(r.shape, r...]
    pallas_call x1, Pallas kernels: 86 us -> 84.8 us  [body(): pl.pallas_call(functools.partial(kernel, n_pipe, n_dp, n_tensor), out_sha...]
where the time goes in v3:
time: 88.2 us; the launch traced here: 88 us
  Pallas kernels  86.1 us (98%)
  between operations  1.29 us (1%)
    pallas_call x1, Pallas kernels, body(): pl.pallas_call(functools.partial(kernel, n_pipe, n_dp, n_tensor), out_sha...  84.8 us

profile of v3, /device:TPU:1, one launch (start us, length us, event | category | flops | bytes accessed | tf_op | source)
XLA Modules:
  0.0 88.0 jit_solution(17970689878503626240)
XLA Ops:
  1.3 0.0 copy-start
  1.3 0.7 copy-done
  2.0 84.8 %shard_map.102 = (bf16[1,128,2048]{2,1,0:T(8,128)(2,1)S(1)}, bf16[1,128,2048]{2,1,0:T(8,128)(2,1)S(1)}, bf16[1,128,2048]{2,1,0:T(8,128)(2,1)S(1)}, f32[1,2048]{1,0:T(1,128)S(1)}) custom-call(s32[1]{0:T(128)S(6)} %copy.11.slot_ref, bf16[1,128,2048]{2,1,0:T(8,128)(2,1)} %out_in.1, bf16[1,128,2048]{2,1,0:T(8,128)(2,1)} %grad_in.1, ...), custom_call_target="tpu_custom_call" | custom-call | tf_op jit(solution)/shard_map/pallas_call | solution.py:296
  86.8 1.2 %shard_map.103 = (bf16[1,128,2048]{2,1,0:T(8,128)(2,1)}, bf16[1,128,2048]{2,1,0:T(8,128)(2,1)}, bf16[1,128,2048]{2,1,0:T(8,128)(2,1)}, f32[1,2048]{1,0:T(1,128)}) custom-call(bf16[1,128,2048]{2,1,0:T(8,128)(2,1)S(1)} %get-tuple-element.8.refs_0_, bf16[1,128,2048]{2,1,0:T(8,128)(2,1)S(1)} %get-tuple-element.9.refs_1_, ...), custom_call_target="tpu_custom_call" | custom-call | tf_op jit(solution)/shard_map/pallas_call | solution.py:317
Async XLA Ops:
  1.3 0.7 copy-start

commit v4 on v3

--- a/solution.py
+++ b/solution.py
@@ -10,7 +10,7 @@
 epsilon = 1e-05
 MESH = pl.DeviceIdType.MESH
 F32, BF16 = jnp.float32, jnp.bfloat16
-TILE = 256
+UP_TILE, WIDE_TILE = 384, 512
 CUTS = 4
 
 
@@ -39,7 +39,8 @@
     width, hidden_units = up.shape
     core = t % 2
     sibling = t + 1 - 2 * core
-    across = [(t + 2 * p) % n_tensor for p in range(1, n_tensor // 2)]
+    steps = sorted(range(1, n_tensor // 2), key=lambda p: min(p, n_tensor // 2 - p))
+    across = [(t + 2 * p) % n_tensor for p in steps]
     peers = [(t + p) % n_tensor for p in range(1, n_tensor)]
     dp_peers = [(d + p) % n_dp for p in range(1, n_dp)]
     after, before = (s + 1) % n_pipe, (s + n_pipe - 1) % n_pipe
@@ -82,7 +83,7 @@
     z_f.start()
 
     def gather_start(which, at):
-        for i, k in enumerate([sibling] + across):
+        for i, k in enumerate(across[::-1] + [sibling]):
             remote(at(t), at(t), ag_send.at[which, i], ag_recv.at[which, t], tensor=k).start()
 
     def gather_pass(which, at):
@@ -95,7 +96,7 @@
             remote(at(k), at(k), ag_send.at[which, 0], ag_recv.at[which, k], tensor=sibling).wait_recv()
 
     def gather_sent(which, at):
-        for i, k in enumerate([sibling] + across):
+        for i, k in enumerate(across[::-1] + [sibling]):
             remote(at(t), at(t), ag_send.at[which, i], ag_recv.at[which, t], tensor=k).wait_send()
         for i, k in enumerate(across):
             remote(at(k), at(k), ag_send.at[which, 4 + i], ag_recv.at[which, k], tensor=sibling).wait_send()
@@ -117,40 +118,41 @@
     norm_f[t] = (rms(fwd_own[...].astype(F32))[0] * gains).astype(BF16)
     gather_start(2, at_f)
 
-    @pl.when(keeper != s)
-    def _():
-        z_t.start()
-
-    @pl.when(keeper == s)
-    def _():
-        l_t.start()
-
     gather_pass(0, at_s)
     gather_pass(1, at_g)
     gather_pass(2, at_f)
+
+    @pl.when(keeper != s)
+    def _():
+        z_t.start()
+
+    @pl.when(keeper == s)
+    def _():
+        l_t.start()
+
     gather_wait(0, at_s)
     gather_wait(1, at_g)
 
     tokens = n_tensor * rows
     nt = (((1,), (1,)), ((), ()))
 
-    def cut(i):
-        return pl.ds(pl.multiple_of(i * TILE, TILE), TILE)
+    def cut(i, tile=UP_TILE):
+        return pl.ds(pl.multiple_of(i * tile, tile), tile)
 
     load_up.wait()
     load_down.wait()
 
-    @pl.loop(0, hidden_units // TILE)
+    @pl.loop(0, hidden_units // UP_TILE)
     def _(i):
         pre = jnp.dot(norm_s[...].reshape(tokens, width), up[:, cut(i)], preferred_element_type=F32)
         back = lax.dot_general(inc[...].reshape(tokens, width), down[cut(i), :], nt, preferred_element_type=F32)
         sigma = jax.nn.sigmoid(pre)
         mid[0, :, cut(i)] = (back * (sigma * (1.0 + pre * (1.0 - sigma)))).astype(BF16)
 
-    @pl.loop(0, width // TILE)
+    @pl.loop(0, width // WIDE_TILE)
     def _(i):
-        part = lax.dot_general(mid[0], up[cut(i), :], nt, preferred_element_type=F32)
-        part_b[:, :, cut(i)] = part.astype(BF16).reshape(n_tensor, rows, TILE)
+        part = lax.dot_general(mid[0], up[cut(i, WIDE_TILE), :], nt, preferred_element_type=F32)
+        part_b[:, :, cut(i, WIDE_TILE)] = part.astype(BF16).reshape(n_tensor, rows, WIDE_TILE)
 
     y_own, y_all = t // 2, n_tensor // 2
     far = [(y_own + p) % y_all for p in sorted(range(1, y_all), key=lambda p: -min(p, y_all - p))]
@@ -189,15 +191,15 @@
     scatter_start(0, part_b, sum_b)
     gather_wait(2, at_f)
 
-    @pl.loop(0, hidden_units // TILE)
+    @pl.loop(0, hidden_units // UP_TILE)
     def _(i):
         pre = jnp.dot(norm_f[...].reshape(tokens, width), up[:, cut(i)], preferred_element_type=F32)
         mid[1, :, cut(i)] = jax.nn.silu(pre).astype(BF16)
 
-    @pl.loop(0, width // TILE)
+    @pl.loop(0, width // WIDE_TILE)
     def _(i):
-        part = jnp.dot(mid[1], down[:, cut(i)], preferred_element_type=F32)
-        part_f[:, :, cut(i)] = part.astype(BF16).reshape(n_tensor, rows, TILE)
+        part = jnp.dot(mid[1], down[:, cut(i, WIDE_TILE)], preferred_element_type=F32)
+        part_f[:, :, cut(i, WIDE_TILE)] = part.astype(BF16).reshape(n_tensor, rows, WIDE_TILE)
 
     scatter_start(1, part_f, sum_f)
 
@@ -213,7 +215,7 @@
     def ends_start(which, end, at):
         keep = pltpu.make_async_copy(end, at(t), local_sem.at[which])
         keep.start()
-        for i, k in enumerate([sibling] + across):
+        for i, k in enumerate(across[::-1] + [sibling]):
             remote(end, at(t), ag_send.at[which, i], ag_recv.at[which, t], tensor=k).start()
         return keep
 

time: 88.2 us -> 87.3 us (0.990)
  Pallas kernels: 86.1 us -> 85.2 us
where the time goes in v4:
time: 87.3 us; the launch traced here: 87.2 us
  Pallas kernels  85.2 us (98%)
  between operations  1.29 us (1%)
    pallas_call x1, Pallas kernels, body(): pl.pallas_call(functools.partial(kernel, n_pipe, n_dp, n_tensor), out_sha...  83.9 us

profile of v4, /device:TPU:1, one launch (start us, length us, event | category | flops | bytes accessed | tf_op | source)
XLA Modules:
  0.0 87.2 jit_solution(3489441041378505439)
XLA Ops:
  1.3 0.0 copy-start
  1.3 0.7 copy-done
  2.0 83.9 %shard_map.102 = (bf16[1,128,2048]{2,1,0:T(8,128)(2,1)S(1)}, bf16[1,128,2048]{2,1,0:T(8,128)(2,1)S(1)}, bf16[1,128,2048]{2,1,0:T(8,128)(2,1)S(1)}, f32[1,2048]{1,0:T(1,128)S(1)}) custom-call(s32[1]{0:T(128)S(6)} %copy.11.slot_ref, bf16[1,128,2048]{2,1,0:T(8,128)(2,1)} %out_in.1, bf16[1,128,2048]{2,1,0:T(8,128)(2,1)} %grad_in.1, ...), custom_call_target="tpu_custom_call" | custom-call | tf_op jit(solution)/shard_map/pallas_call | solution.py:298
  85.9 1.2 %shard_map.103 = (bf16[1,128,2048]{2,1,0:T(8,128)(2,1)}, bf16[1,128,2048]{2,1,0:T(8,128)(2,1)}, bf16[1,128,2048]{2,1,0:T(8,128)(2,1)}, f32[1,2048]{1,0:T(1,128)}) custom-call(bf16[1,128,2048]{2,1,0:T(8,128)(2,1)S(1)} %get-tuple-element.8.refs_0_, bf16[1,128,2048]{2,1,0:T(8,128)(2,1)S(1)} %get-tuple-element.9.refs_1_, ...), custom_call_target="tpu_custom_call" | custom-call | tf_op jit(solution)/shard_map/pallas_call | solution.py:319
Async XLA Ops:
  1.3 0.7 copy-start
